TPU v7x, 32 devices: a whole 2x2x4 slice. The times are simulated.
32 devices in a mesh: dp: 8 (over y, x, core), fsdp: 4 (over z).
Axes of the slice: x: 2, y: 2, z: 4, core: 2. Of those that a mesh axis runs over, the one named last changes fastest.
Arguments:
- layer_input: bfloat16 [4096, 8192], P(('dp', 'fsdp')), may hold values from -24 to 24
- norm_gain: float32 [8192], P('fsdp'), may hold values from 0.4 to 2.4
- value_weight: bfloat16 [8192, 512], P('fsdp'), may hold values from -0.25 to 0.25
- value_cotangent: bfloat16 [4096, 512], P(('dp', 'fsdp')), may hold values from -36 to 36
Outputs:
- input_grad: bfloat16 [4096, 8192], P(('dp', 'fsdp'))
- weight_update: bfloat16 [8192, 512], P('fsdp', 'dp')
- gain_update: bfloat16 [8192], P('fsdp')
All inputs are finite; a program needn't handle non-finite values.
Results may differ from a plain program's by a relative error of at most 0.015.
Values may be sent and summed in bfloat16 or wider, within the bound.
A program may use at most 64 MiB of HBM per device.

v0:
```python
import math

import jax
import jax.numpy as jnp
from jax import lax
from jax.sharding import PartitionSpec as P

EPS_NORM = 1e-05
EPS_SUM = 1e-06


def partner(block, axis, stride):
    count = lax.axis_size(axis)
    route = []
    for low in range(count):
        high = low | 1 << stride
        if high != low and high < count:
            route += [(low, high), (high, low)]
    return lax.ppermute(block, axis, route)


def combine_pair(mine, other, norm_mine, norm_other, inner):
    coef_mine = 1.0 - inner / (2.0 * (norm_mine + EPS_SUM))
    coef_other = 1.0 - inner / (2.0 * (norm_other + EPS_SUM))
    return (coef_mine * mine + coef_other * other).astype(jnp.bfloat16)


def body(layer_input, norm_gain, value_weight, value_cotangent):
    input32 = layer_input.astype(jnp.float32)
    inverse_rms = lax.rsqrt(jnp.mean(input32 * input32, axis=1, keepdims=True) + EPS_NORM)
    normed = input32 * inverse_rms
    normed_b = normed.astype(jnp.bfloat16)
    columns = lax.all_to_all(normed_b, "fsdp", split_axis=1, concat_axis=0, tiled=True)
    cotangent = lax.all_gather(value_cotangent, "fsdp", axis=0, tiled=True)
    grad_scale = 1.0 / math.sqrt(cotangent.shape[0])
    columns32 = columns.astype(jnp.float32)
    scaled = (columns32 * norm_gain[None, :]).astype(jnp.bfloat16)
    grad_w = (
        lax.dot_general(
            scaled, cotangent, (((0,), (0,)), ((), ())), preferred_element_type=jnp.float32
        )
        * grad_scale
    ).astype(jnp.bfloat16)
    back = lax.dot_general(
        cotangent, value_weight, (((1,), (1,)), ((), ())), preferred_element_type=jnp.float32
    )
    grad_g = (jnp.sum(back * columns32, axis=0) * grad_scale).astype(jnp.bfloat16)
    hat_grad = (back * norm_gain[None, :]).astype(jnp.bfloat16)
    returned = lax.all_to_all(hat_grad, "fsdp", split_axis=0, concat_axis=1, tiled=True)
    hat32 = returned.astype(jnp.float32)
    mean_term = jnp.mean(hat32 * normed, axis=1, keepdims=True)
    input_grad = (inverse_rms * (hat32 - normed * mean_term)).astype(jnp.bfloat16)
    levels = lax.axis_size("dp").bit_length() - 1
    replica = lax.axis_index("dp")
    mine_w, mine_g = (grad_w, grad_g)
    for depth_step in range(levels):
        pair_bit = levels - 1 - depth_step
        other_w, other_g = partner((mine_w, mine_g), "dp", pair_bit)
        first_w = mine_w.astype(jnp.float32)
        second_w = other_w.astype(jnp.float32)
        first_g = mine_g.astype(jnp.float32)
        second_g = other_g.astype(jnp.float32)
        totals = lax.psum(
            (
                jnp.sum(first_w * first_w),
                jnp.sum(second_w * second_w),
                jnp.sum(first_w * second_w),
                jnp.sum(first_g * first_g),
                jnp.sum(second_g * second_g),
                jnp.sum(first_g * second_g),
            ),
            "fsdp",
        )
        mine_w = combine_pair(first_w, second_w, totals[0], totals[1], totals[2])
        mine_g = combine_pair(first_g, second_g, totals[3], totals[4], totals[5])
    width_own = mine_w.shape[1] // lax.axis_size("dp")
    weight_update = lax.dynamic_slice_in_dim(mine_w, replica * width_own, width_own, 1)
    return (input_grad, weight_update, mine_g)


def solution(mesh):
    in_specs = (P(("dp", "fsdp"), None), P("fsdp"), P("fsdp", None), P(("dp", "fsdp"), None))
    out_specs = (P(("dp", "fsdp"), None), P("fsdp", "dp"), P("fsdp"))
    return jax.shard_map(body, mesh=mesh, in_specs=in_specs, out_specs=out_specs, check_vma=False)
```

profile of v0, /device:TPU:0, one launch (start us, length us, event | category | flops | bytes accessed | tf_op | source)
XLA Modules:
  0.0 244.6 jit_solution(15705184214816094291)
XLA Ops:
  0.6 0.0 copy-start
  0.6 2.2 fusion.7
  2.9 2.0 fusion
  4.9 0.0 copy-start.6
  4.9 0.0 copy-start.7
  5.0 1.5 copy.12
  6.4 6.3 %all-to-all-start.1 = ((bf16[128,4,2048]{2,0,1:T(8,128)(2,1)}), bf16[128,4,2048]{2,0,1:T(8,128)(2,1)}, u32[]{:S(2)}, u32[]{:S(2)}) async-start(bf16[128,4,2048]{2,0,1:T(8,128)(2,1)} %bitcast.24), calls=%async_computation.1 | async-start | bytes 4194304 | tf_op jit(solution)/shard_map/all_to_all | solution.py:33
  12.7 58.6 %all_gather.3 = bf16[512,512]{1,0:T(8,128)(2,1)S(1)} all-gather(bf16[128,512]{1,0:T(8,128)(2,1)S(1)} %copy-done.6), channel_id=1, replica_groups=mesh['dp'=8,'fsdp'=4] {'fsdp'}, dimensions={0}, use_global_device_ids=true | all-gather | bytes 655360 | tf_op jit(solution)/shard_map/all_gather | solution.py:34
  71.3 0.0 all-to-all-done.1
  71.3 0.0 copy-done.7
  71.3 4.3 %fusion.19 = (f32[2048]{0:T(1024)S(1)}, bf16[512,2048]{1,0:T(8,128)(2,1)}, bf16[512,2048]{1,0:T(8,128)(2,1)S(1)}) fusion(bf16[128,4,2048]{2,0,1:T(8,128)(2,1)} %all-to-all-done.1, f32[2048]{0:T(1024)S(1)} %copy-done.7, bf16[512,512]{1,0:T(8,128)(2,1)S(1)} %all_gather.3, bf16[2048,512]{1,0:T(8,128)(2,1)S(1)} %copy-done), kind=kOutput, calls=%fused_computation.33 | convolution fusion | flops 1081079808 | bytes 8929280 | tf_op jit(solution)/shard_map/dot_general | solution.py:44
  75.6 2.6 %multiply_convert_fusion = bf16[2048,512]{0,1:T(8,128)(2,1)} fusion(bf16[512,2048]{1,0:T(8,128)(2,1)S(1)} %get-tuple-element.43, bf16[512,512]{1,0:T(8,128)(2,1)S(1)} %all_gather.3), kind=kOutput, calls=%fused_computation.38 | convolution fusion | flops 1075838976 | bytes 4718592 | tf_op jit(solution)/shard_map/dot_general | solution.py:39
  78.2 1.5 collective-permute-start
  79.8 4.6 %all-to-all-start = ((bf16[4,128,2048]{2,1,0:T(8,128)(2,1)}), bf16[4,128,2048]{2,1,0:T(8,128)(2,1)}, u32[]{:S(2)}, u32[]{:S(2)}) async-start(bf16[4,128,2048]{2,1,0:T(8,128)(2,1)} %bitcast.26), calls=%async_computation | async-start | bytes 4194304 | tf_op jit(solution)/shard_map/all_to_all | solution.py:49
  84.4 0.5 collective-permute-start.3
  84.9 38.0 %collective-permute-done.3 = bf16[2048]{0:T(1024)(128)(2,1)S(1)} collective-permute-done((bf16[2048]{0:T(1024)(128)(2,1)S(1)}, bf16[2048]{0:T(1024)(128)(2,1)S(1)}, u32[]{:S(2)}, u32[]{:S(2)}) %collective-permute-start.3) | collective-permute-done | bytes 4128 | tf_op jit(solution)/shard_map/ppermute | solution.py:19
  122.9 0.7 fusion.22
  123.5 0.0 collective-permute-done
  123.5 3.9 %fusion.8 = (f32[]{:T(128)}, f32[]{:T(128)}, f32[]{:T(128)}) fusion(bf16[2048,512]{0,1:T(8,128)(2,1)} %multiply_convert_fusion, bf16[2048,512]{0,1:T(8,128)(2,1)} %collective-permute-done), kind=kLoop, calls=%fused_computation.20 | loop fusion | flops 8388605 | bytes 4194316 | tf_op jit(solution)/shard_map/reduce_sum | solution.py:65
  127.4 11.8 %all-reduce.2 = (f32[]{:T(128)}, f32[]{:T(128)}, f32[]{:T(128)}, f32[]{:T(128)}, f32[]{:T(128)}, /*index=5*/f32[]{:T(128)}) all-reduce(f32[]{:T(128)} %get-tuple-element.10, f32[]{:T(128)} %get-tuple-element.11, f32[]{:T(128)} %get-tuple-element.9, f32[]{:T(128)} %get-tuple-element.19, ...), channel_id=1, replica_groups=mesh['dp'=8,'fsdp'=4] {'fsdp'}, use_global_device_ids=true, to_apply=%region_3.0 | all-reduce | flops 6 | bytes 48 | tf_op jit(solution)/shard_map/psum | solution.py:63
  141.8 4.5 %fusion.10 = bf16[2048,512]{0,1:T(8,128)(2,1)} fusion(bf16[2048,512]{0,1:T(8,128)(2,1)} %multiply_convert_fusion, bf16[2048,512]{0,1:T(8,128)(2,1)} %collective-permute-done, f32[]{:T(128)S(6)} %sub.41, f32[]{:T(128)S(6)} %sub.40), kind=kLoop, calls=%fused_computation.22 | loop fusion | flops 6291456 | bytes 6291464 | tf_op jit(solution)/shard_map/convert_element_type | solution.py:25
  146.3 1.5 collective-permute-start.1
  150.4 0.6 collective-permute-start.4
  151.0 36.5 %collective-permute-done.4 = bf16[2048]{0:T(1024)(128)(2,1)S(1)} collective-permute-done((bf16[2048]{0:T(1024)(128)(2,1)S(1)}, bf16[2048]{0:T(1024)(128)(2,1)S(1)}, u32[]{:S(2)}, u32[]{:S(2)}) %collective-permute-start.4) | collective-permute-done | bytes 4128 | tf_op jit(solution)/shard_map/ppermute | solution.py:19
  187.5 0.6 fusion.27
  188.1 0.0 all-to-all-done
  188.1 2.1 convert_bitcast_fusion
  190.2 0.0 copy-start.3
  190.2 0.5 copy.10
  190.7 1.3 copy-done.3
  192.1 0.7 fusion.3
  192.8 0.0 collective-permute-done.1
  192.8 3.9 %fusion.13 = (f32[]{:T(128)}, f32[]{:T(128)}, f32[]{:T(128)}) fusion(bf16[2048,512]{0,1:T(8,128)(2,1)} %fusion.10, bf16[2048,512]{0,1:T(8,128)(2,1)} %collective-permute-done.1), kind=kLoop, calls=%fused_computation.25 | loop fusion | flops 8388605 | bytes 4194316 | tf_op jit(solution)/shard_map/reduce_sum | solution.py:65
  196.7 9.3 %all-reduce.1 = (f32[]{:T(128)}, f32[]{:T(128)}, f32[]{:T(128)}, f32[]{:T(128)}, f32[]{:T(128)}, /*index=5*/f32[]{:T(128)}) all-reduce(f32[]{:T(128)} %get-tuple-element.7, f32[]{:T(128)} %get-tuple-element.8, f32[]{:T(128)} %get-tuple-element.6, f32[]{:T(128)} %get-tuple-element.16, ...), channel_id=1, replica_groups=mesh['dp'=8,'fsdp'=4] {'fsdp'}, use_global_device_ids=true, to_apply=%region_9.0 | all-reduce | flops 6 | bytes 48 | tf_op jit(solution)/shard_map/psum | solution.py:63
  211.0 0.0 copy-start.4
  211.0 0.1 collective-permute-start.5
  211.1 5.3 %fusion.37 = (f32[2048,512]{0,1:T(8,128)}, bf16[2048,512]{0,1:T(8,128)(2,1)S(1)}) fusion(bf16[2048,512]{0,1:T(8,128)(2,1)} %collective-permute-done.1, f32[]{:T(128)S(6)} %sub.43, bf16[2048,512]{0,1:T(8,128)(2,1)} %fusion.10, f32[]{:T(128)S(6)} %sub.42), kind=kLoop, calls=%fused_computation.78 | loop fusion | flops 7340032 | bytes 10485768 | tf_op jit(solution)/shard_map/convert_element_type | solution.py:59
  216.4 0.3 collective-permute-start.2
  216.7 2.3 fusion.6
  219.0 0.0 collective-permute-done.5
  219.0 0.7 fusion.32
  219.7 0.9 collective-permute-done.2
  220.6 1.3 copy-done.5
  221.9 1.9 multiply_reduce_fusion.1
  223.8 11.0 %all-reduce = (f32[]{:T(128)}, f32[]{:T(128)}, f32[]{:T(128)}, f32[]{:T(128)}, f32[]{:T(128)}, /*index=5*/f32[]{:T(128)}) all-reduce(f32[]{:T(128)} %get-tuple-element.4, f32[]{:T(128)} %get-tuple-element.5, f32[]{:T(128)} %get-tuple-element.3, f32[]{:T(128)} %get-tuple-element.13, ...), channel_id=1, replica_groups=mesh['dp'=8,'fsdp'=4] {'fsdp'}, use_global_device_ids=true, to_apply=%region_15.0 | all-reduce | flops 6 | bytes 48 | tf_op jit(solution)/shard_map/psum | solution.py:63
  240.0 2.1 convert_element_type.112
  242.1 1.8 fusion.21
  244.0 0.6 fusion.34
  (13 shorter events, 0.1 us)
Async XLA Ops:
  0.6 70.7 %copy-start = (bf16[2048,512]{1,0:T(8,128)(2,1)S(1)}, bf16[2048,512]{1,0:T(8,128)(2,1)}, u32[]{:S(2)}) copy-start(bf16[2048,512]{1,0:T(8,128)(2,1)} %param.6) | copy-start | bytes 6291460
  4.9 7.8 %copy-start.6 = (bf16[128,512]{1,0:T(8,128)(2,1)S(1)}, bf16[128,512]{1,0:T(8,128)(2,1)}, u32[]{:S(2)}) copy-start(bf16[128,512]{1,0:T(8,128)(2,1)} %param.7) | copy-start | bytes 393220
  4.9 66.4 %copy-start.7 = (f32[2048]{0:T(1024)S(1)}, f32[2048]{0:T(1024)}, u32[]{:S(2)}) copy-start(f32[2048]{0:T(1024)} %param.5) | copy-start | bytes 24580
  6.4 64.9 %all-to-all-start.1 = ((bf16[128,4,2048]{2,0,1:T(8,128)(2,1)}), bf16[128,4,2048]{2,0,1:T(8,128)(2,1)}, u32[]{:S(2)}, u32[]{:S(2)}) async-start(bf16[128,4,2048]{2,0,1:T(8,128)(2,1)} %bitcast.24), calls=%async_computation.1 | async-start | bytes 4194304 | tf_op jit(solution)/shard_map/all_to_all | solution.py:33
  78.2 45.3 %collective-permute-start = (bf16[2048,512]{0,1:T(8,128)(2,1)}, bf16[2048,512]{0,1:T(8,128)(2,1)}, u32[]{:S(2)}, u32[]{:S(2)}) collective-permute-start(bf16[2048,512]{0,1:T(8,128)(2,1)} %multiply_convert_fusion), channel_id=1, source_target_pairs={{0,16},{16,0},{4,20},{20,4},{8,24},{24,8},{12,28},{28,12},{1,17},{... | collective-permute-start | bytes 6291464 | tf_op jit(solution)/shard_map/ppermute | solution.py:19
  79.8 108.3 %all-to-all-start = ((bf16[4,128,2048]{2,1,0:T(8,128)(2,1)}), bf16[4,128,2048]{2,1,0:T(8,128)(2,1)}, u32[]{:S(2)}, u32[]{:S(2)}) async-start(bf16[4,128,2048]{2,1,0:T(8,128)(2,1)} %bitcast.26), calls=%async_computation | async-start | bytes 4194304 | tf_op jit(solution)/shard_map/all_to_all | solution.py:49
  84.4 38.5 %collective-permute-start.3 = (bf16[2048]{0:T(1024)(128)(2,1)S(1)}, bf16[2048]{0:T(1024)(128)(2,1)S(1)}, u32[]{:S(2)}, u32[]{:S(2)}) collective-permute-start(bf16[2048]{0:T(1024)(128)(2,1)S(1)} %multiply_convert_fusion.2), channel_id=1, source_target_pairs={{0,16},{16,0},{4,20},{20,4},{8,24},{24,8},{12,28},{28,12},{1,17},{... | collective-permute-start | bytes 12296 | tf_op jit(solution)/shard_map/ppermute | solution.py:19
  146.3 46.5 %collective-permute-start.1 = (bf16[2048,512]{0,1:T(8,128)(2,1)}, bf16[2048,512]{0,1:T(8,128)(2,1)}, u32[]{:S(2)}, u32[]{:S(2)}) collective-permute-start(bf16[2048,512]{0,1:T(8,128)(2,1)} %fusion.10), channel_id=1, source_target_pairs={{0,8},{8,0},{4,12},{12,4},{16,24},{24,16},{20,28},{28,20},{1,9},{9... | collective-permute-start | bytes 6291464 | tf_op jit(solution)/shard_map/ppermute | solution.py:19
  150.4 37.1 %collective-permute-start.4 = (bf16[2048]{0:T(1024)(128)(2,1)S(1)}, bf16[2048]{0:T(1024)(128)(2,1)S(1)}, u32[]{:S(2)}, u32[]{:S(2)}) collective-permute-start(bf16[2048]{0:T(1024)(128)(2,1)S(1)} %fusion.24), channel_id=1, source_target_pairs={{0,8},{8,0},{4,12},{12,4},{16,24},{24,16},{20,28},{28,20},{1,9},{9... | collective-permute-start | bytes 12296 | tf_op jit(solution)/shard_map/ppermute | solution.py:19
  190.2 1.9 copy-start.3
  190.7 6.0 %copy-start.1 = (f32[4,16,8,2048]{3,2,0,1:T(8,128)}, f32[4,16,8,2048]{3,2,0,1:T(8,128)S(1)}, u32[]{:S(2)}) copy-start(f32[4,16,8,2048]{3,2,0,1:T(8,128)S(1)} %copy.10) | copy-start | bytes 12582916
  211.0 5.8 %copy-start.2 = (f32[4,16,8,2048]{3,2,0,1:T(8,128)S(1)}, f32[4,16,8,2048]{3,2,0,1:T(8,128)}, u32[]{:S(2)}) copy-start(f32[4,16,8,2048]{3,2,0,1:T(8,128)} %copy-done.1) | copy-start | bytes 12582916
  211.0 5.8 %copy-start.4 = (bf16[128,8192]{1,0:T(8,128)(2,1)S(1)}, bf16[128,8192]{1,0:T(8,128)(2,1)}, u32[]{:S(2)}) copy-start(bf16[128,8192]{1,0:T(8,128)(2,1)} %param.4) | copy-start | bytes 6291460
  211.0 8.0 %collective-permute-start.5 = (bf16[2048]{0:T(1024)(128)(2,1)S(1)}, bf16[2048]{0:T(1024)(128)(2,1)S(1)}, u32[]{:S(2)}, u32[]{:S(2)}) collective-permute-start(bf16[2048]{0:T(1024)(128)(2,1)S(1)} %fusion.29), channel_id=1, source_target_pairs={{0,4},{4,0},{8,12},{12,8},{16,20},{20,16},{24,28},{28,24},{1,5},{5... | collective-permute-start | bytes 12296 | tf_op jit(solution)/shard_map/ppermute | solution.py:19
  216.4 4.2 %collective-permute-start.2 = (bf16[2048,512]{0,1:T(8,128)(2,1)S(1)}, bf16[2048,512]{0,1:T(8,128)(2,1)S(1)}, u32[]{:S(2)}, u32[]{:S(2)}) collective-permute-start(bf16[2048,512]{0,1:T(8,128)(2,1)S(1)} %get-tuple-element.40), channel_id=1, source_target_pairs={{0,4},{4,0},{8,12},{12,8},{16,20},{20,16},{24,28},{28,24},{1,5},{5... | collective-permute-start | bytes 6291464 | tf_op jit(solution)/shard_map/ppermute | solution.py:19
  220.6 1.3 copy-start.5
where the time goes:
time: 245 us
  blocking collectives  90.7 us (37%)
  waiting for transfers between devices  75.3 us (31%)
  other arithmetic  35.6 us (15%)
  between operations  16 us (7%)
  starting transfers between devices  15.4 us (6%)
  matrix products  6.91 us (3%)
  local copies, waits for them, and re-layouts  4.65 us (2%)
    ppermute x6, waiting for transfers between devices, partner(): return lax.ppermute(block, axis, route)  75.3 us
    all_gather x1, blocking collectives, body(): cotangent = lax.all_gather(value_cotangent, 'fsdp', axis=0, tiled=True)  58.6 us
    psum x3, blocking collectives, body(): lax.psum((jnp.sum(first_w * first_w), jnp.sum(second_w * second_w), jnp.s...  32.1 us
    reduce_sum x3, other arithmetic, body(): jnp.sum(first_w * first_w)  9.76 us
    convert_element_type x5, other arithmetic, combine_pair(): return (coef_mine * mine + coef_other * other).astype(jnp.bfloat16)  6.99 us
    all_to_all x1, starting transfers between devices, body(): lax.all_to_all(normed_b, 'fsdp', split_axis=1, concat_axis=0, tiled=True)  6.32 us
    convert_element_type x1, other arithmetic, body(): first_w = mine_w.astype(jnp.float32)  5.33 us
  transfers between devices with their start and end apart: 8, of which 3 were waited for; matrix products, arithmetic and copies ran while one was open for 9% of the time, Pallas kernels for 0%

commit v1 on v0

v1 whole, which is shorter than its diff:
```python
import math

import jax
import jax.numpy as jnp
from jax import lax
from jax.sharding import PartitionSpec as P

EPS_NORM = 1e-05
EPS_SUM = 1e-06


def coefficients(gram):
    count = gram.shape[-1]
    levels = count.bit_length() - 1
    eye = jnp.eye(count, dtype=jnp.float32)
    coef = jnp.broadcast_to(eye, gram.shape)
    for depth_step in range(levels):
        stride = 1 << (levels - 1 - depth_step)

        def swap(block, axis):
            shape = block.shape
            split = shape[:axis] + (count // (2 * stride), 2, stride) + shape[axis + 1 :]
            return jnp.flip(block.reshape(split), axis + 1).reshape(shape)

        norm = jnp.maximum(jnp.sum(gram * eye, axis=-1), 0.0)
        inner = jnp.sum(gram * swap(eye, 0), axis=-1)
        mine = 1.0 - inner / (2.0 * (norm + EPS_SUM))
        other = swap(mine, 1)
        coef = mine[..., None] * coef + other[..., None] * swap(coef, 1)
        gram = mine[..., None] * gram + other[..., None] * swap(gram, 1)
        gram = mine[..., None, :] * gram + other[..., None, :] * swap(gram, 2)
    return coef[..., 0, :]


def body(layer_input, norm_gain, value_weight, value_cotangent):
    input32 = layer_input.astype(jnp.float32)
    inverse_rms = lax.rsqrt(jnp.mean(input32 * input32, axis=1, keepdims=True) + EPS_NORM)
    normed = input32 * inverse_rms
    normed_b = normed.astype(jnp.bfloat16)
    columns = lax.all_to_all(normed_b, "fsdp", split_axis=1, concat_axis=0, tiled=True)
    cotangent = lax.all_gather(value_cotangent, "fsdp", axis=0, tiled=True)
    grad_scale = 1.0 / math.sqrt(cotangent.shape[0])
    columns32 = columns.astype(jnp.float32)
    scaled = (columns32 * norm_gain[None, :]).astype(jnp.bfloat16)
    grad_w = (
        lax.dot_general(
            cotangent, scaled, (((0,), (0,)), ((), ())), preferred_element_type=jnp.float32
        )
        * grad_scale
    ).astype(jnp.bfloat16)
    back = lax.dot_general(
        cotangent, value_weight, (((1,), (1,)), ((), ())), preferred_element_type=jnp.float32
    )
    grad_g = (jnp.sum(back * columns32, axis=0) * grad_scale).astype(jnp.bfloat16)
    hat_grad = (back * norm_gain[None, :]).astype(jnp.bfloat16)
    returned = lax.all_to_all(hat_grad, "fsdp", split_axis=0, concat_axis=1, tiled=True)
    hat32 = returned.astype(jnp.float32)
    mean_term = jnp.mean(hat32 * normed, axis=1, keepdims=True)
    input_grad = (inverse_rms * (hat32 - normed * mean_term)).astype(jnp.bfloat16)
    count = lax.axis_size("dp")
    own = grad_w.shape[0] // count
    slabs = lax.all_to_all(grad_w, "dp", split_axis=0, concat_axis=0, tiled=True)
    all_g = lax.all_gather(grad_g, "dp", axis=0).astype(jnp.float32)
    products = lax.dot_general(slabs, slabs, (((1,), (1,)), ((), ())), preferred_element_type=jnp.float32)
    products = products.reshape(count, own, count, own)
    gram_w = jnp.sum(products * jnp.eye(own, dtype=jnp.float32)[None, :, None, :], axis=(1, 3))
    gram_g = jnp.sum(all_g[:, None, :] * all_g[None, :, :], axis=2) / count
    coef = coefficients(lax.psum(jnp.stack([gram_w, gram_g]), ("dp", "fsdp")))
    slabs32 = slabs.reshape(count, own, -1).astype(jnp.float32)
    weight = jnp.sum(coef[0][:, None, None] * slabs32, axis=0).astype(jnp.bfloat16)
    gain = jnp.sum(coef[1][:, None] * all_g, axis=0).astype(jnp.bfloat16)
    return (input_grad, weight.T, gain)


def solution(mesh):
    in_specs = (P(("dp", "fsdp"), None), P("fsdp"), P("fsdp", None), P(("dp", "fsdp"), None))
    out_specs = (P(("dp", "fsdp"), None), P("fsdp", "dp"), P("fsdp"))
    return jax.shard_map(body, mesh=mesh, in_specs=in_specs, out_specs=out_specs, check_vma=False)
```

time: 245 us -> 197 us (0.80)
  waiting for transfers between devices: 75.3 us -> 0.01 us
  blocking collectives: 90.7 us -> 151 us
  other arithmetic: 35.6 us -> 12.6 us
  between operations: 16 us -> 0.83 us
  matrix products: 6.91 us -> 11.6 us
    ppermute x6 -> x0, waiting for transfers between devices: 75.3 us -> none  [partner(): return lax.ppermute(block, axis, route)]
    psum x3 -> x1, blocking collectives: 32.1 us -> 63.4 us  [body(): coef = coefficients(lax.psum(jnp.stack([gram_w, gram_g]), ('dp', 'fsdp')))]
    all_gather x0 -> x1, blocking collectives: none -> 29.4 us  [body(): all_g = lax.all_gather(grad_g, 'dp', axis=0).astype(jnp.float32)]
    convert_element_type x7, other arithmetic: 14.4 us -> 0.37 us  [the longest x6 0.36 us: coefficients(): eye = jnp.eye(count, dtype=jnp.float32)]
    reduce_sum x6, other arithmetic: 11.7 us -> 3.93 us  [the longest x1 2.85 us: body(): jnp.sum(coef[0][:, None, None] * slabs32, axis=0).astype(jnp.bfloat16)]
    dot_general x1 -> x2, matrix products: 2.61 us -> 7.33 us  [the longest x1 4.72 us: body(): lax.dot_general(slabs, slabs, (((1,), (1,)), ((), ())), preferred_element...]
    ppermute x6 -> x0, starting transfers between devices: 4.52 us -> none  [partner(): return lax.ppermute(block, axis, route)]
    all_to_all x0 -> x1, starting transfers between devices: none -> 4.34 us  [body(): lax.all_to_all(grad_w, 'dp', split_axis=0, concat_axis=0, tiled=True)]
  transfers between devices with their start and end apart: 8 -> 3, of which waited for: 3 -> 0; matrix products, arithmetic and copies ran while one was open for 9% -> 6% of each run, Pallas kernels for 0% -> 0%
where the time goes in v1:
time: 197 us
  blocking collectives  151 us (77%)
  starting transfers between devices  15.4 us (8%)
  other arithmetic  12.6 us (6%)
  matrix products  11.6 us (6%)
  local copies, waits for them, and re-layouts  4.67 us (2%)
    psum x1, blocking collectives, body(): coef = coefficients(lax.psum(jnp.stack([gram_w, gram_g]), ('dp', 'fsdp')))  63.4 us
    all_gather x1, blocking collectives, body(): cotangent = lax.all_gather(value_cotangent, 'fsdp', axis=0, tiled=True)  58.6 us
    all_gather x1, blocking collectives, body(): all_g = lax.all_gather(grad_g, 'dp', axis=0).astype(jnp.float32)  29.4 us
    all_to_all x1, starting transfers between devices, body(): lax.all_to_all(normed_b, 'fsdp', split_axis=1, concat_axis=0, tiled=True)  6.45 us
    dot_general x1, matrix products, body(): lax.dot_general(slabs, slabs, (((1,), (1,)), ((), ())), preferred_element...  4.72 us
    all_to_all x1, starting transfers between devices, body(): lax.all_to_all(hat_grad, 'fsdp', split_axis=0, concat_axis=1, tiled=True)  4.62 us
    all_to_all x1, starting transfers between devices, body(): lax.all_to_all(grad_w, 'dp', split_axis=0, concat_axis=0, tiled=True)  4.34 us
    dot_general x1, matrix products, body(): lax.dot_general(cotangent, value_weight, (((1,), (1,)), ((), ())), prefer...  4.31 us
  transfers between devices with their start and end apart: 3, of which 0 were waited for; matrix products, arithmetic and copies ran while one was open for 6% of the time, Pallas kernels for 0%

profile of v1, /device:TPU:0, one launch (start us, length us, event | category | flops | bytes accessed | tf_op | source)
XLA Modules:
  0.0 196.6 jit_solution(2823598872227426366)
XLA Ops:
  0.7 2.2 %fusion.7 = f32[128]{0:T(128)S(1)} fusion(bf16[128,8192]{1,0:T(8,128)(2,1)} %param.4), kind=kLoop, calls=%fused_computation.9 | loop fusion | flops 3145600 | bytes 2097664 | tf_op jit(solution)/shard_map/reduce_sum | solution.py:37
  2.9 0.1 copy-done.1
  3.0 0.4 fusion
  3.5 1.5 copy.44
  4.9 6.4 %all-to-all-start.1 = ((bf16[128,4,2048]{2,0,1:T(8,128)(2,1)}), bf16[128,4,2048]{2,0,1:T(8,128)(2,1)}, u32[]{:S(2)}, u32[]{:S(2)}) async-start(bf16[128,4,2048]{2,0,1:T(8,128)(2,1)} %bitcast.74), calls=%async_computation.1 | async-start | bytes 4194304 | tf_op jit(solution)/shard_map/all_to_all | solution.py:40
  11.4 58.6 %all_gather.7 = bf16[512,512]{1,0:T(8,128)(2,1)S(1)} all-gather(bf16[128,512]{1,0:T(8,128)(2,1)S(1)} %copy-done.3), channel_id=1, replica_groups=mesh['dp'=8,'fsdp'=4] {'fsdp'}, dimensions={0}, use_global_device_ids=true | all-gather | bytes 655360 | tf_op jit(solution)/shard_map/all_gather | solution.py:41
  70.0 4.3 %fusion.9 = (f32[2048]{0:T(1024)S(1)}, bf16[512,2048]{1,0:T(8,128)(2,1)}, bf16[512,2048]{1,0:T(8,128)(2,1)S(1)}) fusion(bf16[128,4,2048]{2,0,1:T(8,128)(2,1)} %all-to-all-done.1, f32[2048]{0:T(1024)S(1)} %copy-done.4, bf16[512,512]{1,0:T(8,128)(2,1)S(1)} %all_gather.7, bf16[2048,512]{1,0:T(8,128)(2,1)S(1)} %copy-done), kind=kOutput, calls=%fused_computation.13 | convolution fusion | flops 1081079808 | bytes 8929280 | tf_op jit(solution)/shard_map/dot_general | solution.py:51
  74.4 2.6 %multiply_convert_fusion = bf16[2048,512]{0,1:T(8,128)(2,1)} fusion(bf16[512,2048]{1,0:T(8,128)(2,1)S(1)} %get-tuple-element.18, bf16[512,512]{1,0:T(8,128)(2,1)S(1)} %all_gather.7), kind=kOutput, calls=%fused_computation.16 | convolution fusion | flops 1075838976 | bytes 4718592 | tf_op jit(solution)/shard_map/dot_general | solution.py:46
  77.0 4.3 %all-to-all-start.2 = ((bf16[8,64,2048]{2,1,0:T(8,128)(2,1)}), bf16[8,64,2048]{2,1,0:T(8,128)(2,1)}, u32[]{:S(2)}, u32[]{:S(2)}) async-start(bf16[8,64,2048]{2,1,0:T(8,128)(2,1)} %bitcast.77), calls=%async_computation.2 | async-start | bytes 4194304 | tf_op jit(solution)/shard_map/all_to_all | solution.py:62
  81.3 0.1 compare_convert_fusion.1
  81.4 0.1 fusion.18
  81.6 0.1 compare_convert_fusion
  81.7 29.4 %all-gather = bf16[16384]{0:T(1024)(128)(2,1)S(1)} all-gather(bf16[2048]{0:T(1024)(128)(2,1)S(1)} %multiply_convert_fusion.2), channel_id=2, replica_groups=mesh['dp'=8,'fsdp'=4] {'dp'}, dimensions={0}, use_global_device_ids=true | all-gather | bytes 36864 | tf_op jit(solution)/shard_map/all_gather | solution.py:63
  111.1 0.1 multiply_reduce_fusion.2
  111.3 4.6 %all-to-all-start = ((bf16[4,128,2048]{2,1,0:T(8,128)(2,1)}), bf16[4,128,2048]{2,1,0:T(8,128)(2,1)}, u32[]{:S(2)}, u32[]{:S(2)}) async-start(bf16[4,128,2048]{2,1,0:T(8,128)(2,1)} %bitcast.76), calls=%async_computation | async-start | bytes 4194304 | tf_op jit(solution)/shard_map/all_to_all | solution.py:56
  115.9 4.7 %multiply_reduce_fusion.1 = f32[8,8]{1,0:T(8,128)S(1)} fusion(bf16[8,64,2048]{2,1,0:T(8,128)(2,1)} %all-to-all-done.2, f32[64,64]{1,0:T(8,128)S(1)} %fusion.17), kind=kOutput, calls=%fused_computation.22 | convolution fusion | flops 1074266112 | bytes 2113792 | tf_op jit(solution)/shard_map/dot_general | solution.py:64
  120.6 63.4 %psum.7 = f32[2,8,8]{2,1,0:T(8,128)S(1)} all-reduce(f32[2,8,8]{2,1,0:T(8,128)S(1)} %pad_maximum_fusion), channel_id=1, replica_groups=mesh['dp'=8,'fsdp'=4] {'dp','fsdp'}, use_global_device_ids=true, to_apply=%region_5.0 | all-reduce | flops 128 | bytes 1024 | tf_op jit(solution)/shard_map/psum | solution.py:68
  184.1 0.1 multiply_reduce_fusion.8
  184.2 0.1 div.85
  184.3 0.1 mul.415
  184.4 0.1 mul.456
  184.4 0.1 mul.446
  184.5 0.1 reshape.446
  184.6 0.1 reshape.442
  184.7 0.1 multiply_add_fusion.2
  184.8 0.1 multiply_add_fusion.6
  184.9 0.1 copy.33
  185.0 0.1 copy.34
  185.0 0.1 multiply_reduce_fusion.6
  185.1 0.1 div.87
  185.3 0.1 mul.429
  185.4 0.1 reshape.444
  185.4 0.1 multiply_add_fusion.1
  185.6 0.1 multiply_add_fusion.4
  185.7 0.1 copy.35
  185.8 0.1 copy.36
  185.8 0.1 multiply_reduce_fusion.4
  185.9 0.1 div.90
  186.0 0.1 reverse.11
  186.1 0.1 mul.451
  186.2 0.1 multiply_add_fusion
  186.3 0.7 multiply_reduce_fusion.3
  187.0 2.8 %multiply_reduce_fusion = bf16[64,2048]{1,0:T(8,128)(2,1)} fusion(bf16[8,64,2048]{2,1,0:T(8,128)(2,1)} %all-to-all-done.2, f32[8]{0:T(128)S(1)} %get-tuple-element.20), kind=kLoop, calls=%fused_computation.15 | loop fusion | flops 3014656 | bytes 2359328 | tf_op jit(solution)/shard_map/reduce_sum | solution.py:70
  189.9 2.1 %convert_bitcast_fusion = f32[4,16,8,2048]{3,2,1,0:T(8,128)S(1)} fusion(bf16[4,128,2048]{2,1,0:T(8,128)(2,1)} %all-to-all-done), kind=kLoop, calls=%fused_computation.14 | loop fusion | flops 1048576 | bytes 6291456
  192.0 0.3 copy.42
  192.3 1.3 copy-done.2
  193.6 0.7 fusion.3
  194.3 2.3 %fusion.6 = bf16[128,8192]{1,0:T(8,128)(2,1)} fusion(f32[128,8192]{1,0:T(8,128)S(1)} %bitcast.73, bf16[128,8192]{1,0:T(8,128)(2,1)S(1)} %copy-done.2, f32[128]{0:T(128)S(1)} %broadcast_multiply_fusion, f32[128]{0:T(128)S(1)} %add_rsqrt_fusion), kind=kLoop, calls=%fused_computation.8 | loop fusion | flops 6291456 | bytes 8389632 | tf_op jit(solution)/shard_map/convert_element_type | solution.py:59
  (44 shorter events, 0.5 us)
Async XLA Ops:
  0.6 69.4 %copy-start = (bf16[2048,512]{1,0:T(8,128)(2,1)S(1)}, bf16[2048,512]{1,0:T(8,128)(2,1)}, u32[]{:S(2)}) copy-start(bf16[2048,512]{1,0:T(8,128)(2,1)} %param.6) | copy-start | bytes 6291460
  0.6 2.4 %copy-start.1 = (bf16[128,8192]{1,0:T(8,128)(2,1)S(1)}, bf16[128,8192]{1,0:T(8,128)(2,1)}, u32[]{:S(2)}) copy-start(bf16[128,8192]{1,0:T(8,128)(2,1)} %param.4) | copy-start | bytes 6291460
  4.9 6.5 %copy-start.3 = (bf16[128,512]{1,0:T(8,128)(2,1)S(1)}, bf16[128,512]{1,0:T(8,128)(2,1)}, u32[]{:S(2)}) copy-start(bf16[128,512]{1,0:T(8,128)(2,1)} %param.7) | copy-start | bytes 393220
  4.9 65.1 %copy-start.4 = (f32[2048]{0:T(1024)S(1)}, f32[2048]{0:T(1024)}, u32[]{:S(2)}) copy-start(f32[2048]{0:T(1024)} %param.5) | copy-start | bytes 24580
  4.9 65.1 %all-to-all-start.1 = ((bf16[128,4,2048]{2,0,1:T(8,128)(2,1)}), bf16[128,4,2048]{2,0,1:T(8,128)(2,1)}, u32[]{:S(2)}, u32[]{:S(2)}) async-start(bf16[128,4,2048]{2,0,1:T(8,128)(2,1)} %bitcast.74), calls=%async_computation.1 | async-start | bytes 4194304 | tf_op jit(solution)/shard_map/all_to_all | solution.py:40
  77.0 34.3 %all-to-all-start.2 = ((bf16[8,64,2048]{2,1,0:T(8,128)(2,1)}), bf16[8,64,2048]{2,1,0:T(8,128)(2,1)}, u32[]{:S(2)}, u32[]{:S(2)}) async-start(bf16[8,64,2048]{2,1,0:T(8,128)(2,1)} %bitcast.77), calls=%async_computation.2 | async-start | bytes 4194304 | tf_op jit(solution)/shard_map/all_to_all | solution.py:62
  111.3 78.6 %all-to-all-start = ((bf16[4,128,2048]{2,1,0:T(8,128)(2,1)}), bf16[4,128,2048]{2,1,0:T(8,128)(2,1)}, u32[]{:S(2)}, u32[]{:S(2)}) async-start(bf16[4,128,2048]{2,1,0:T(8,128)(2,1)} %bitcast.76), calls=%async_computation | async-start | bytes 4194304 | tf_op jit(solution)/shard_map/all_to_all | solution.py:56
  192.0 1.6 copy-start.2

commit v2 on v1

v2 whole, which is shorter than its diff:
```python
import functools
import math

import jax
import jax.numpy as jnp
from jax import lax
from jax.experimental import pallas as pl
from jax.experimental.pallas import tpu as pltpu
from jax.sharding import PartitionSpec as P

EPS_NORM = 1e-05
EPS_SUM = 1e-06
MESH = pl.DeviceIdType.MESH
F32 = jnp.float32
BF16 = jnp.bfloat16


def dot_t(a, b):
    return lax.dot_general(a, b, (((1,), (1,)), ((), ())), preferred_element_type=F32)


def coefficients(gram):
    count, lanes = gram.shape
    row = lax.broadcasted_iota(jnp.int32, gram.shape, 0)
    lane = lax.broadcasted_iota(jnp.int32, gram.shape, 1)
    coef = jnp.where(row == lane, 1.0, 0.0).astype(F32)
    stride = count // 2
    while stride:
        row_set = lax.rem(row // stride, 2) == 1
        lane_set = lax.rem(lane // stride, 2) == 1
        row_partner = jnp.where(row_set, row - stride, row + stride)

        def swap_rows(block):
            down = pltpu.roll(block, stride, 0)
            up = pltpu.roll(block, count - stride, 0)
            return jnp.where(row_set, down, up)

        def swap_lanes(block):
            down = pltpu.roll(block, stride, 1)
            up = pltpu.roll(block, lanes - stride, 1)
            return jnp.where(lane_set, down, up)

        own = jnp.where(row == lane, gram, 0.0)
        meet = jnp.where(row_partner == lane, gram, 0.0)

        def weights(axis):
            norm = jnp.maximum(jnp.sum(own, axis=axis, keepdims=True), 0.0)
            inner = jnp.sum(meet, axis=axis, keepdims=True)
            return jnp.broadcast_to(1.0 - inner / (2.0 * (norm + EPS_SUM)), gram.shape)

        mine, mine_lane = weights(1), weights(0)
        other, other_lane = swap_rows(mine), swap_lanes(mine_lane)
        coef = mine * coef + other * swap_rows(coef)
        gram = mine * gram + other * swap_rows(gram)
        gram = mine_lane * gram + other_lane * swap_lanes(gram)
        stride //= 2
    return coef


def kernel(
    n_d, n_f, n_k,
    x_ref, gain_ref, w_ref, cot_ref,
    ig_ref, wu_ref, gu_ref,
    inv, nb, cols, cot_all, gain_all, wall, gsend, slabs, products, g_own, g_all, gram1, gram2,
    w_send, w_recv, c_send, c_recv, n_send, n_recv, col_send, col_recv, hyp_send, hyp_recv,
    slab_send, slab_recv, g_send, g_recv, one_send, one_recv, two_send, two_recv,
):
    d, f = lax.axis_index("dp"), lax.axis_index("fsdp")
    tok, model = x_ref.shape
    owned, width = w_ref.shape
    chunk = owned // n_k
    rows = owned // n_d
    slab = width // n_d
    scale = 1.0 / math.sqrt(n_f * tok)
    sent = []

    def f_peer(o):
        return (d, lax.rem(f + o, n_f))

    def d_peer(o):
        return (lax.rem(d + o, n_d), f)

    def send(src, dst, send_sem, recv_sem, device):
        copy = pltpu.make_async_remote_copy(
            src_ref=src, dst_ref=dst, send_sem=send_sem, recv_sem=recv_sem,
            device_id=device, device_id_type=MESH,
        )
        copy.start()
        sent.append(copy)
        return copy

    def features(o, k):
        return pl.ds(pl.multiple_of(lax.rem(f + o, n_f) * owned + k * chunk, 128), chunk)

    barrier = pltpu.get_barrier_semaphore()
    for o in range(1, n_f):
        pl.semaphore_signal(barrier, inc=1, device_id=f_peer(o), device_id_type=MESH)
    for o in range(1, n_d):
        pl.semaphore_signal(barrier, inc=1, device_id=d_peer(o), device_id_type=MESH)

    def square(step, total):
        part = x_ref[:, pl.ds(pl.multiple_of(step * 512, 512), 512)].astype(F32)
        part = part * part
        for at in range(0, 512, 128):
            total = total + part[:, at : at + 128]
        return total

    squares = lax.fori_loop(0, model // 512, square, jnp.zeros((tok, 128), F32))
    mean = jnp.sum(squares, axis=1, keepdims=True) / model
    inv[...] = jnp.broadcast_to(lax.rsqrt(mean + EPS_NORM), inv.shape)
    pl.semaphore_wait(barrier, n_f + n_d - 2)

    own_rows = pl.ds(pl.multiple_of(d * rows, 16), rows)
    first, cot_copies, gain_copies = [], [], []
    for o in range(1, n_f):
        at = n_f - o
        first.append(
            send(w_ref.at[own_rows], wall.at[d, at - 1], w_send.at[o - 1], w_recv.at[at - 1], f_peer(o))
        )
    for o in range(1, n_f):
        at = n_f - o
        cot_copies.append(
            send(cot_ref, cot_all.at[at], c_send.at[o - 1], c_recv.at[at - 1], f_peer(o))
        )
        gain_copies.append(
            send(gain_ref, gain_all.at[at], n_send.at[o - 1], n_recv.at[at - 1], f_peer(o))
        )
    cot_all[0] = cot_ref[...]
    gain_all[0] = gain_ref[...]

    col_copies = []
    for k in range(n_k):
        copies = []
        for o in range(n_f):
            normed = (x_ref[:, features(o, k)].astype(F32) * inv[:, :1]).astype(BF16)
            if o == 0:
                cols[k, 0] = normed
                continue
            at = n_f - o
            nb[k, o - 1] = normed
            copies.append(
                send(nb.at[k, o - 1], cols.at[k, at], col_send.at[k, o - 1], col_recv.at[k, at - 1], f_peer(o))
            )
        col_copies.append(copies)

    half = width // 2
    bits = [1 << b for b in reversed(range(n_d.bit_length() - 1))]
    orders = [bits, bits[1::-1] + bits[2:]]
    pending = [first, []]

    def flip(mask):
        index = d
        for bit in bits:
            if mask & bit:
                index = index + bit * (1 - 2 * lax.rem(d // bit, 2))
        return index

    def spread(level):
        for copy in pending[0]:
            copy.wait_recv()
        pending[0] = []
        if level == len(bits):
            return
        for part, order in enumerate(orders):
            held = [0]
            for bit in order[:level]:
                held = held + [mask ^ bit for mask in held]
            bit = order[level]
            for mask in held:
                place = wall.at[flip(mask), :, :, pl.ds(part * half, half)]
                pending[0].append(
                    send(
                        place, place, hyp_send.at[part, (mask ^ bit) - 1], hyp_recv.at[part, (mask ^ bit) - 1],
                        (flip(bit), f),
                    )
                )

    def input_gradient():
        def back_part(o, k):
            if o == 0:
                block = w_ref[k * chunk : (k + 1) * chunk]
            else:
                group = chunk // rows
                block = wall[k * group : (k + 1) * group, o - 1].reshape(chunk, width)
            back = dot_t(cot_ref[...], block)
            return (back * gain_all[o, :, k * chunk : (k + 1) * chunk]).astype(BF16)

        total = jnp.zeros((tok, 128), F32)
        for o in range(n_f):
            for k in range(n_k):
                hat = back_part(o, k)
                place = features(o, k)
                ig_ref[:, place] = hat
                term = hat.astype(F32) * (x_ref[:, place].astype(F32) * inv[:, :1])
                for at in range(0, chunk, 128):
                    total = total + term[:, at : at + 128]
        mean_term = jnp.sum(total, axis=1, keepdims=True) / model

        def finish(step, carry):
            place = pl.ds(pl.multiple_of(step * 512, 512), 512)
            normed = x_ref[:, place].astype(F32) * inv[:, :1]
            hat32 = ig_ref[:, place].astype(F32)
            ig_ref[:, place] = (inv[:, :1] * (hat32 - normed * mean_term)).astype(BF16)
            return carry

        lax.fori_loop(0, model // 512, finish, 0)

    slab_copies = []

    def gather_products(k):
        for copy in slab_copies[k]:
            copy.wait_recv()
        block = slabs[k].reshape(width, chunk)
        if k == 0:
            products[...] = dot_t(block, block)
        else:
            products[...] += dot_t(block, block)

    spread(0)
    for copy in cot_copies + gain_copies:
        copy.wait_recv()
    for k in range(n_k):
        if k == n_k - 1:
            for level in range(min(n_k, len(bits) + 1), len(bits) + 1):
                spread(level)
            input_gradient()
        for copy in col_copies[k]:
            copy.wait_recv()
        place = slice(k * chunk, (k + 1) * chunk)
        cotangent = cot_all[...].reshape(n_f * tok, width)
        columns32 = cols[k].reshape(n_f * tok, chunk).astype(F32)
        scaled = (columns32 * gain_ref[:, place]).astype(BF16)
        grad = lax.dot_general(cotangent, scaled, (((0,), (0,)), ((), ())), preferred_element_type=F32)
        gsend[k] = (grad * scale).astype(BF16).reshape(n_d, slab, chunk)
        copies = []
        for o in range(1, n_d):
            copies.append(
                send(
                    gsend.at[k, lax.rem(d + o, n_d)], slabs.at[k, d],
                    slab_send.at[k, o - 1], slab_recv.at[k, n_d - o - 1], d_peer(o),
                )
            )
        slab_copies.append(copies)
        slabs[k, d] = gsend[k, d]
        back = dot_t(cotangent, w_ref[place])
        gain_grad = jnp.sum(back * columns32, axis=0, keepdims=True) * scale
        g_own[:, place] = gain_grad.astype(BF16).astype(F32)
        if k + 1 < n_k:
            spread(k + 1) if k + 1 <= len(bits) else None
        if k:
            gather_products(k - 1)

    g_copies = []
    for o in range(1, n_d):
        g_copies.append(send(g_own, g_all.at[d], g_send.at[o - 1], g_recv.at[n_d - o - 1], d_peer(o)))
    g_all[d] = g_own[...]
    gather_products(n_k - 1)

    row = lax.broadcasted_iota(jnp.int32, (width, width), 0)
    lane = lax.broadcasted_iota(jnp.int32, (width, width), 1)
    same = lax.rem(row, slab) == lax.rem(lane, slab)
    by_row = jnp.sum(jnp.where(same, products[...], 0.0).reshape(n_d, slab, width), axis=1)
    column = lax.broadcasted_iota(jnp.int32, (n_d, 128), 1)
    gram_w = jnp.zeros((n_d, 128), F32)
    for s in range(n_d):
        part = jnp.sum(by_row[:, s * slab : (s + 1) * slab], axis=1, keepdims=True)
        gram_w = jnp.where(column == s, part, gram_w)
    gram1[d] = gram_w
    one_copies = []
    for o in range(1, n_d):
        one_copies.append(
            send(gram1.at[d], gram1.at[d], one_send.at[o - 1], one_recv.at[n_d - o - 1], d_peer(o))
        )
    for copy in g_copies:
        copy.wait_recv()
    gains = g_all[...].reshape(n_d, owned)
    gram_g = jnp.zeros((n_d, 128), F32)
    for s in range(n_d):
        part = jnp.sum(gains * gains[s : s + 1], axis=1, keepdims=True)
        gram_g = jnp.where(column == s, part, gram_g)
    for copy in one_copies:
        copy.wait_recv()
    total = gram1[0]
    for s in range(1, n_d):
        total = total + gram1[s]
    gram2[f, 0] = total
    gram2[f, 1] = gram_g
    two_copies = []
    for o in range(1, n_f):
        two_copies.append(
            send(gram2.at[f], gram2.at[f], two_send.at[o - 1], two_recv.at[n_f - o - 1], f_peer(o))
        )
    for copy in two_copies:
        copy.wait_recv()
    sum_w, sum_g = gram2[0, 0], gram2[0, 1]
    for s in range(1, n_f):
        sum_w = sum_w + gram2[s, 0]
        sum_g = sum_g + gram2[s, 1]
    coef_w, coef_g = coefficients(sum_w), coefficients(sum_g)
    gain_total = coef_g[0:1, 0:1] * gains[0:1]
    for s in range(1, n_d):
        gain_total = gain_total + coef_g[0:1, s : s + 1] * gains[s : s + 1]
    gu_ref[...] = gain_total.astype(BF16)
    for k in range(n_k):
        weight_total = coef_w[0:1, 0:1] * slabs[k, 0].astype(F32)
        for s in range(1, n_d):
            weight_total = weight_total + coef_w[0:1, s : s + 1] * slabs[k, s].astype(F32)
        wu_ref[:, k * chunk : (k + 1) * chunk] = weight_total.astype(BF16)
    for copy in sent:
        copy.wait_send()


def body(n_d, n_f, layer_input, norm_gain, value_weight, value_cotangent):
    tok, model = layer_input.shape
    owned, width = value_weight.shape
    chunk = min(512, owned)
    n_k = owned // chunk
    rows, slab = owned // n_d, width // n_d
    dma = pltpu.SemaphoreType.DMA
    vmem = pl.BlockSpec(memory_space=pltpu.VMEM)
    pairs = [(n_f - 1,)] * 6 + [(n_k, n_f - 1)] * 2 + [(2, n_d - 1)] * 2 + [(n_k, n_d - 1)] * 2
    pairs += [(n_d - 1,)] * 4 + [(n_f - 1,)] * 2
    input_grad, weight, gain = pl.pallas_call(
        functools.partial(kernel, n_d, n_f, n_k),
        out_shape=(
            jax.ShapeDtypeStruct((tok, model), BF16),
            jax.ShapeDtypeStruct((slab, owned), BF16),
            jax.ShapeDtypeStruct((1, owned), BF16),
        ),
        in_specs=[vmem] * 4,
        out_specs=(vmem,) * 3,
        scratch_shapes=[
            pltpu.VMEM((tok, 128), F32),
            pltpu.VMEM((n_k, n_f - 1, tok, chunk), BF16),
            pltpu.VMEM((n_k, n_f, tok, chunk), BF16),
            pltpu.VMEM((n_f, tok, width), BF16),
            pltpu.VMEM((n_f, 1, owned), F32),
            pltpu.VMEM((n_d, n_f - 1, rows, width), BF16),
            pltpu.VMEM((n_k, n_d, slab, chunk), BF16),
            pltpu.VMEM((n_k, n_d, slab, chunk), BF16),
            pltpu.VMEM((width, width), F32),
            pltpu.VMEM((1, owned), F32),
            pltpu.VMEM((n_d, 1, owned), F32),
            pltpu.VMEM((n_d, n_d, 128), F32),
            pltpu.VMEM((n_f, 2, n_d, 128), F32),
        ]
        + [dma(shape) for shape in pairs],
        compiler_params=pltpu.CompilerParams(
            collective_id=0, has_side_effects=True, vmem_limit_bytes=56 * 1024 * 1024
        ),
        cost_estimate=pl.CostEstimate(
            flops=8 * tok * model * width, bytes_accessed=8 * tok * model, transcendentals=0
        ),
    )(layer_input, norm_gain.reshape(1, owned), value_weight, value_cotangent)
    return (input_grad, weight.T, gain.reshape(owned))


def solution(mesh):
    in_specs = (P(("dp", "fsdp"), None), P("fsdp"), P("fsdp", None), P(("dp", "fsdp"), None))
    out_specs = (P(("dp", "fsdp"), None), P("fsdp", "dp"), P("fsdp"))
    inner = functools.partial(body, mesh.shape["dp"], mesh.shape["fsdp"])
    return jax.shard_map(inner, mesh=mesh, in_specs=in_specs, out_specs=out_specs, check_vma=False)
```

time: 197 us -> 134 us (0.68)
  blocking collectives: 151 us -> 0 us
  Pallas kernels: 0 us -> 128 us
  starting transfers between devices: 15.4 us -> 0 us
  matrix products: 11.6 us -> 0 us
  other arithmetic: 12.6 us -> 1.32 us
    pallas_call x0 -> x1, Pallas kernels: none -> 128 us  [body(): pl.pallas_call(functools.partial(kernel, n_d, n_f, n_k), out_shape=(jax.S...]
    all_gather x2 -> x0, blocking collectives: 88 us -> none  [the longest x1 58.6 us: body(): cotangent = lax.all_gather(value_cotangent, 'fsdp', axis=0, tiled=True)]
    psum x1 -> x0, blocking collectives: 63.4 us -> none  [body(): coef = coefficients(lax.psum(jnp.stack([gram_w, gram_g]), ('dp', 'fsdp')))]
    all_to_all x3 -> x0, starting transfers between devices: 15.4 us -> none  [the longest x1 6.45 us: body(): lax.all_to_all(normed_b, 'fsdp', split_axis=1, concat_axis=0, tiled=True)]
    dot_general x3 -> x0, matrix products: 11.6 us -> none  [the longest x1 4.72 us: body(): lax.dot_general(slabs, slabs, (((1,), (1,)), ((), ())), preferred_element...]
    reduce_sum x8 -> x0, other arithmetic: 6.9 us -> none  [the longest x1 2.85 us: body(): jnp.sum(coef[0][:, None, None] * slabs32, axis=0).astype(jnp.bfloat16)]
    convert_element_type x10 -> x0, other arithmetic: 3.11 us -> none  [the longest x1 2.29 us: body(): (inverse_rms * (hat32 - normed * mean_term)).astype(jnp.bfloat16)]
    unnamed x10 -> x4, local copies, waits for them, and re-layouts: 1.45 us -> 3.84 us
  transfers between devices with their start and end apart: 3 -> 0, of which waited for: 0 -> 0; matrix products, arithmetic and copies ran while one was open for 6% -> 0% of each run, Pallas kernels for 0% -> 0%
where the time goes in v2:
time: 134 us
  Pallas kernels  128 us (96%)
  local copies, waits for them, and re-layouts  3.84 us (3%)
    pallas_call x1, Pallas kernels, body(): pl.pallas_call(functools.partial(kernel, n_d, n_f, n_k), out_shape=(jax.S...  128 us
    unnamed x4, local copies, waits for them, and re-layouts  3.84 us

profile of v2, /device:TPU:0, one launch (start us, length us, event | category | flops | bytes accessed | tf_op | source)
XLA Modules:
  0.0 133.9 jit_solution(10631039713024974414)
XLA Ops:
  0.6 128.1 %shard_map.67 = (bf16[128,8192]{1,0:T(8,128)(2,1)}, bf16[64,2048]{1,0:T(8,128)(2,1)}, bf16[1,2048]{1,0:T(2,128)(2,1)}) custom-call(bf16[128,8192]{1,0:T(8,128)(2,1)} %x_ref.1, f32[1,2048]{1,0:T(1,128)} %bitcast.3, bf16[2048,512]{1,0:T(8,128)(2,1)} %w_ref.1, bf16[128,512]{1,0:T(8,128)(2,1)} %cot_ref.1), custom_call_target="tpu_custom_call" | custom-call | flops 4294967296 | bytes 8388608 | tf_op jit(solution)/shard_map/pallas_call | solution.py:323
  128.8 1.3 reduce
  130.1 0.0 copy-start
  130.1 3.1 %copy.9 = bf16[128,8192]{1,0:T(8,128)(2,1)} copy(bf16[128,8192]{1,0:T(8,128)(2,1)} %get-tuple-element.12) | data formatting | bytes 4194304
  133.2 0.0 copy-done
  133.2 0.7 copy.10
Async XLA Ops:
  130.1 3.1 %copy-start = (bf16[64,2048]{1,0:T(8,128)(2,1)S(1)}, bf16[64,2048]{1,0:T(8,128)(2,1)}, u32[]{:S(2)}) copy-start(bf16[64,2048]{1,0:T(8,128)(2,1)} %get-tuple-element.7) | copy-start | bytes 786436

commit v3 on v2

--- a/solution.py
+++ b/solution.py
@@ -61,7 +61,7 @@
     n_d, n_f, n_k,
     x_ref, gain_ref, w_ref, cot_ref,
     ig_ref, wu_ref, gu_ref,
-    inv, nb, cols, cot_all, gain_all, wall, gsend, slabs, products, g_own, g_all, gram1, gram2,
+    inv, nb, cols, cot_all, gain_all, wall, gsend, slabs, cot_turned, products, g_own, g_all, gram1, gram2,
     w_send, w_recv, c_send, c_recv, n_send, n_recv, col_send, col_recv, hyp_send, hyp_recv,
     slab_send, slab_recv, g_send, g_recv, one_send, one_recv, two_send, two_recv,
 ):
@@ -89,6 +89,11 @@
         sent.append(copy)
         return copy
 
+    def left(copies):
+        for copy in copies:
+            copy.wait_send()
+        sent[:] = [copy for copy in sent if all(copy is not gone for gone in copies)]
+
     def features(o, k):
         return pl.ds(pl.multiple_of(lax.rem(f + o, n_f) * owned + k * chunk, 128), chunk)
 
@@ -130,14 +135,17 @@
 
     col_copies = []
     for k in range(n_k):
-        copies = []
         for o in range(n_f):
             normed = (x_ref[:, features(o, k)].astype(F32) * inv[:, :1]).astype(BF16)
             if o == 0:
                 cols[k, 0] = normed
-                continue
+            else:
+                nb[k, o - 1] = normed
+
+    def send_columns(k):
+        copies = []
+        for o in range(1, n_f):
             at = n_f - o
-            nb[k, o - 1] = normed
             copies.append(
                 send(nb.at[k, o - 1], cols.at[k, at], col_send.at[k, o - 1], col_recv.at[k, at - 1], f_peer(o))
             )
@@ -216,13 +224,22 @@
         else:
             products[...] += dot_t(block, block)
 
+    levels = len(bits)
     spread(0)
+    send_columns(0)
+    spread(1)
+    done = 1
     for copy in cot_copies + gain_copies:
         copy.wait_recv()
+    cot_turned[...] = cot_all[...].reshape(n_f * tok, width).T
     for k in range(n_k):
+        if k + 1 < n_k:
+            left(col_copies[k])
+            send_columns(k + 1)
         if k == n_k - 1:
-            for level in range(min(n_k, len(bits) + 1), len(bits) + 1):
-                spread(level)
+            while done < levels:
+                done += 1
+                spread(done)
             input_gradient()
         for copy in col_copies[k]:
             copy.wait_recv()
@@ -230,7 +247,7 @@
         cotangent = cot_all[...].reshape(n_f * tok, width)
         columns32 = cols[k].reshape(n_f * tok, chunk).astype(F32)
         scaled = (columns32 * gain_ref[:, place]).astype(BF16)
-        grad = lax.dot_general(cotangent, scaled, (((0,), (0,)), ((), ())), preferred_element_type=F32)
+        grad = jnp.dot(cot_turned[...], scaled, preferred_element_type=F32)
         gsend[k] = (grad * scale).astype(BF16).reshape(n_d, slab, chunk)
         copies = []
         for o in range(1, n_d):
@@ -245,8 +262,9 @@
         back = dot_t(cotangent, w_ref[place])
         gain_grad = jnp.sum(back * columns32, axis=0, keepdims=True) * scale
         g_own[:, place] = gain_grad.astype(BF16).astype(F32)
-        if k + 1 < n_k:
-            spread(k + 1) if k + 1 <= len(bits) else None
+        if 0 < k < n_k - 1 and done < levels:
+            done += 1
+            spread(done)
         if k:
             gather_products(k - 1)
 
@@ -338,6 +356,7 @@
             pltpu.VMEM((n_d, n_f - 1, rows, width), BF16),
             pltpu.VMEM((n_k, n_d, slab, chunk), BF16),
             pltpu.VMEM((n_k, n_d, slab, chunk), BF16),
+            pltpu.VMEM((width, n_f * tok), BF16),
             pltpu.VMEM((width, width), F32),
             pltpu.VMEM((1, owned), F32),
             pltpu.VMEM((n_d, 1, owned), F32),

time: 134 us -> 114 us (0.85)
  Pallas kernels: 128 us -> 108 us
    pallas_call x1, Pallas kernels: 128 us -> 108 us  [body(): pl.pallas_call(functools.partial(kernel, n_d, n_f, n_k), out_shape=(jax.S...]
where the time goes in v3:
time: 114 us
  Pallas kernels  108 us (95%)
  local copies, waits for them, and re-layouts  3.84 us (3%)
  other arithmetic  1.32 us (1%)
    pallas_call x1, Pallas kernels, body(): pl.pallas_call(functools.partial(kernel, n_d, n_f, n_k), out_shape=(jax.S...  108 us
    unnamed x4, local copies, waits for them, and re-layouts  3.84 us

profile of v3, /device:TPU:0, one launch (start us, length us, event | category | flops | bytes accessed | tf_op | source)
XLA Modules:
  0.0 113.9 jit_solution(11546822463837499036)
XLA Ops:
  0.6 108.1 %shard_map.67 = (bf16[128,8192]{1,0:T(8,128)(2,1)}, bf16[64,2048]{1,0:T(8,128)(2,1)}, bf16[1,2048]{1,0:T(2,128)(2,1)}) custom-call(bf16[128,8192]{1,0:T(8,128)(2,1)} %x_ref.1, f32[1,2048]{1,0:T(1,128)} %bitcast.3, bf16[2048,512]{1,0:T(8,128)(2,1)} %w_ref.1, bf16[128,512]{1,0:T(8,128)(2,1)} %cot_ref.1), custom_call_target="tpu_custom_call" | custom-call | flops 4294967296 | bytes 8388608 | tf_op jit(solution)/shard_map/pallas_call | solution.py:341
  108.7 1.3 %reduce = bf16[2048]{0:T(1024)(128)(2,1)} reduce(bf16[1,2048]{1,0:T(2,128)(2,1)} %get-tuple-element.8, bf16[]{:T(256)} %constant), dimensions={0}, to_apply=%get-tuple-element.8.reduce_sub_computation | reduce | bytes 8194 | tf_op jit(solution)/shard_map/pallas_call | solution.py:341
  110.0 0.0 copy-start
  110.0 3.1 %copy.9 = bf16[128,8192]{1,0:T(8,128)(2,1)} copy(bf16[128,8192]{1,0:T(8,128)(2,1)} %get-tuple-element.12) | data formatting | bytes 4194304
  113.2 0.0 copy-done
  113.2 0.7 copy.10
Async XLA Ops:
  110.0 3.1 %copy-start = (bf16[64,2048]{1,0:T(8,128)(2,1)S(1)}, bf16[64,2048]{1,0:T(8,128)(2,1)}, u32[]{:S(2)}) copy-start(bf16[64,2048]{1,0:T(8,128)(2,1)} %get-tuple-element.7) | copy-start | bytes 786436

commit v4 on v2

--- a/solution.py
+++ b/solution.py
@@ -60,8 +60,8 @@
 def kernel(
     n_d, n_f, n_k,
     x_ref, gain_ref, w_ref, cot_ref,
-    ig_ref, wu_ref, gu_ref,
-    inv, nb, cols, cot_all, gain_all, wall, gsend, slabs, products, g_own, g_all, gram1, gram2,
+    hat_ref, inv, mean_ref, wu_ref, gu_ref,
+    nb, cols, cot_all, gain_all, wall, gsend, slabs, cot_turned, products, g_own, g_all, gram1, gram2,
     w_send, w_recv, c_send, c_recv, n_send, n_recv, col_send, col_recv, hyp_send, hyp_recv,
     slab_send, slab_recv, g_send, g_recv, one_send, one_recv, two_send, two_recv,
 ):
@@ -89,6 +89,11 @@
         sent.append(copy)
         return copy
 
+    def left(copies):
+        for copy in copies:
+            copy.wait_send()
+        sent[:] = [copy for copy in sent if all(copy is not gone for gone in copies)]
+
     def features(o, k):
         return pl.ds(pl.multiple_of(lax.rem(f + o, n_f) * owned + k * chunk, 128), chunk)
 
@@ -97,6 +102,26 @@
         pl.semaphore_signal(barrier, inc=1, device_id=f_peer(o), device_id_type=MESH)
     for o in range(1, n_d):
         pl.semaphore_signal(barrier, inc=1, device_id=d_peer(o), device_id_type=MESH)
+
+    pl.semaphore_wait(barrier, n_f + n_d - 2)
+
+    own_rows = pl.ds(pl.multiple_of(d * rows, 16), rows)
+    first, cot_copies, gain_copies = [], [], []
+    for o in range(1, n_f):
+        at = n_f - o
+        first.append(
+            send(w_ref.at[own_rows], wall.at[d, at - 1], w_send.at[o - 1], w_recv.at[at - 1], f_peer(o))
+        )
+    for o in range(1, n_f):
+        at = n_f - o
+        cot_copies.append(
+            send(cot_ref, cot_all.at[at], c_send.at[o - 1], c_recv.at[at - 1], f_peer(o))
+        )
+        gain_copies.append(
+            send(gain_ref, gain_all.at[at], n_send.at[o - 1], n_recv.at[at - 1], f_peer(o))
+        )
+    cot_all[0] = cot_ref[...]
+    gain_all[0] = gain_ref[...]
 
     def square(step, total):
         part = x_ref[:, pl.ds(pl.multiple_of(step * 512, 512), 512)].astype(F32)
@@ -108,28 +133,10 @@
     squares = lax.fori_loop(0, model // 512, square, jnp.zeros((tok, 128), F32))
     mean = jnp.sum(squares, axis=1, keepdims=True) / model
     inv[...] = jnp.broadcast_to(lax.rsqrt(mean + EPS_NORM), inv.shape)
-    pl.semaphore_wait(barrier, n_f + n_d - 2)
-
-    own_rows = pl.ds(pl.multiple_of(d * rows, 16), rows)
-    first, cot_copies, gain_copies = [], [], []
-    for o in range(1, n_f):
-        at = n_f - o
-        first.append(
-            send(w_ref.at[own_rows], wall.at[d, at - 1], w_send.at[o - 1], w_recv.at[at - 1], f_peer(o))
-        )
-    for o in range(1, n_f):
-        at = n_f - o
-        cot_copies.append(
-            send(cot_ref, cot_all.at[at], c_send.at[o - 1], c_recv.at[at - 1], f_peer(o))
-        )
-        gain_copies.append(
-            send(gain_ref, gain_all.at[at], n_send.at[o - 1], n_recv.at[at - 1], f_peer(o))
-        )
-    cot_all[0] = cot_ref[...]
-    gain_all[0] = gain_ref[...]
 
     col_copies = []
-    for k in range(n_k):
+
+    def send_columns(k):
         copies = []
         for o in range(n_f):
             normed = (x_ref[:, features(o, k)].astype(F32) * inv[:, :1]).astype(BF16)
@@ -175,7 +182,7 @@
                     )
                 )
 
-    def input_gradient():
+    def hat_gradient():
         def back_part(o, k):
             if o == 0:
                 block = w_ref[k * chunk : (k + 1) * chunk]
@@ -190,20 +197,12 @@
             for k in range(n_k):
                 hat = back_part(o, k)
                 place = features(o, k)
-                ig_ref[:, place] = hat
+                hat_ref[:, place] = hat
                 term = hat.astype(F32) * (x_ref[:, place].astype(F32) * inv[:, :1])
                 for at in range(0, chunk, 128):
                     total = total + term[:, at : at + 128]
         mean_term = jnp.sum(total, axis=1, keepdims=True) / model
-
-        def finish(step, carry):
-            place = pl.ds(pl.multiple_of(step * 512, 512), 512)
-            normed = x_ref[:, place].astype(F32) * inv[:, :1]
-            hat32 = ig_ref[:, place].astype(F32)
-            ig_ref[:, place] = (inv[:, :1] * (hat32 - normed * mean_term)).astype(BF16)
-            return carry
-
-        lax.fori_loop(0, model // 512, finish, 0)
+        mean_ref[...] = jnp.broadcast_to(mean_term, mean_ref.shape)
 
     slab_copies = []
 
@@ -216,21 +215,26 @@
         else:
             products[...] += dot_t(block, block)
 
+    levels = len(bits)
+    send_columns(0)
+    if n_k > 1:
+        send_columns(1)
     spread(0)
+    done = 0
     for copy in cot_copies + gain_copies:
         copy.wait_recv()
+    cot_turned[...] = cot_all[...].reshape(n_f * tok, width).T
     for k in range(n_k):
-        if k == n_k - 1:
-            for level in range(min(n_k, len(bits) + 1), len(bits) + 1):
-                spread(level)
-            input_gradient()
         for copy in col_copies[k]:
             copy.wait_recv()
+        if k + 2 < n_k:
+            left(col_copies[k])
+            send_columns(k + 2)
         place = slice(k * chunk, (k + 1) * chunk)
         cotangent = cot_all[...].reshape(n_f * tok, width)
         columns32 = cols[k].reshape(n_f * tok, chunk).astype(F32)
         scaled = (columns32 * gain_ref[:, place]).astype(BF16)
-        grad = lax.dot_general(cotangent, scaled, (((0,), (0,)), ((), ())), preferred_element_type=F32)
+        grad = jnp.dot(cot_turned[...], scaled, preferred_element_type=F32)
         gsend[k] = (grad * scale).astype(BF16).reshape(n_d, slab, chunk)
         copies = []
         for o in range(1, n_d):
@@ -245,8 +249,9 @@
         back = dot_t(cotangent, w_ref[place])
         gain_grad = jnp.sum(back * columns32, axis=0, keepdims=True) * scale
         g_own[:, place] = gain_grad.astype(BF16).astype(F32)
-        if k + 1 < n_k:
-            spread(k + 1) if k + 1 <= len(bits) else None
+        if done < levels:
+            done += 1
+            spread(done)
         if k:
             gather_products(k - 1)
 
@@ -254,6 +259,10 @@
     for o in range(1, n_d):
         g_copies.append(send(g_own, g_all.at[d], g_send.at[o - 1], g_recv.at[n_d - o - 1], d_peer(o)))
     g_all[d] = g_own[...]
+    while done < levels:
+        done += 1
+        spread(done)
+    hat_gradient()
     gather_products(n_k - 1)
 
     row = lax.broadcasted_iota(jnp.int32, (width, width), 0)
@@ -300,7 +309,8 @@
     gain_total = coef_g[0:1, 0:1] * gains[0:1]
     for s in range(1, n_d):
         gain_total = gain_total + coef_g[0:1, s : s + 1] * gains[s : s + 1]
-    gu_ref[...] = gain_total.astype(BF16)
+    for at in range(owned // 128):
+        gu_ref[at : at + 1] = gain_total[:, at * 128 : (at + 1) * 128]
     for k in range(n_k):
         weight_total = coef_w[0:1, 0:1] * slabs[k, 0].astype(F32)
         for s in range(1, n_d):
@@ -320,17 +330,18 @@
     vmem = pl.BlockSpec(memory_space=pltpu.VMEM)
     pairs = [(n_f - 1,)] * 6 + [(n_k, n_f - 1)] * 2 + [(2, n_d - 1)] * 2 + [(n_k, n_d - 1)] * 2
     pairs += [(n_d - 1,)] * 4 + [(n_f - 1,)] * 2
-    input_grad, weight, gain = pl.pallas_call(
+    hat, inverse_rms, mean_term, weight, gain = pl.pallas_call(
         functools.partial(kernel, n_d, n_f, n_k),
         out_shape=(
             jax.ShapeDtypeStruct((tok, model), BF16),
+            jax.ShapeDtypeStruct((tok, 128), F32),
+            jax.ShapeDtypeStruct((tok, 128), F32),
             jax.ShapeDtypeStruct((slab, owned), BF16),
-            jax.ShapeDtypeStruct((1, owned), BF16),
+            jax.ShapeDtypeStruct((owned // 128, 128), F32),
         ),
         in_specs=[vmem] * 4,
-        out_specs=(vmem,) * 3,
+        out_specs=(vmem,) * 5,
         scratch_shapes=[
-            pltpu.VMEM((tok, 128), F32),
             pltpu.VMEM((n_k, n_f - 1, tok, chunk), BF16),
             pltpu.VMEM((n_k, n_f, tok, chunk), BF16),
             pltpu.VMEM((n_f, tok, width), BF16),
@@ -338,6 +349,7 @@
             pltpu.VMEM((n_d, n_f - 1, rows, width), BF16),
             pltpu.VMEM((n_k, n_d, slab, chunk), BF16),
             pltpu.VMEM((n_k, n_d, slab, chunk), BF16),
+            pltpu.VMEM((width, n_f * tok), BF16),
             pltpu.VMEM((width, width), F32),
             pltpu.VMEM((1, owned), F32),
             pltpu.VMEM((n_d, 1, owned), F32),
@@ -352,7 +364,10 @@
             flops=8 * tok * model * width, bytes_accessed=8 * tok * model, transcendentals=0
         ),
     )(layer_input, norm_gain.reshape(1, owned), value_weight, value_cotangent)
-    return (input_grad, weight.T, gain.reshape(owned))
+    inverse_rms = inverse_rms[:, :1]
+    normed = layer_input.astype(F32) * inverse_rms
+    input_grad = (inverse_rms * (hat.astype(F32) - normed * mean_term[:, :1])).astype(BF16)
+    return (input_grad, weight.T, gain.reshape(owned).astype(BF16))
 
 
 def solution(mesh):

time: 134 us -> 120 us (0.90)
  Pallas kernels: 128 us -> 113 us
  other arithmetic: 1.32 us -> 4.55 us
  local copies, waits for them, and re-layouts: 3.84 us -> 1.69 us
    pallas_call x1, Pallas kernels: 128 us -> 113 us  [body(): pl.pallas_call(functools.partial(kernel, n_d, n_f, n_k), out_shape=(jax.S...]
    convert_element_type x0 -> x2, other arithmetic: none -> 4.55 us  [the longest x1 3.96 us: body(): (inverse_rms * (hat.astype(F32) - normed * mean_term[:, :1])).astype(BF16)]
    unnamed x4 -> x7, local copies, waits for them, and re-layouts: 3.84 us -> 0.72 us
where the time goes in v4:
time: 120 us
  Pallas kernels  113 us (94%)
  other arithmetic  4.55 us (4%)
  local copies, waits for them, and re-layouts  1.69 us (1%)
    pallas_call x1, Pallas kernels, body(): pl.pallas_call(functools.partial(kernel, n_d, n_f, n_k), out_shape=(jax.S...  113 us
    convert_element_type x1, other arithmetic, body(): (inverse_rms * (hat.astype(F32) - normed * mean_term[:, :1])).astype(BF16)  3.96 us

profile of v4, /device:TPU:0, one launch (start us, length us, event | category | flops | bytes accessed | tf_op | source)
XLA Modules:
  0.0 120.2 jit_solution(9706209786636671276)
XLA Ops:
  0.6 0.0 copy-start
  0.6 113.3 %shard_map.67 = (bf16[128,8192]{1,0:T(8,128)(2,1)}, f32[128,128]{1,0:T(8,128)}, f32[128,128]{1,0:T(8,128)}, bf16[64,2048]{1,0:T(8,128)(2,1)}, f32[16,128]{1,0:T(8,128)}) custom-call(bf16[128,8192]{1,0:T(8,128)(2,1)} %x_ref.1, f32[1,2048]{1,0:T(1,128)} %bitcast.5, bf16[2048,512]{1,0:T(8,128)(2,1)} %w_ref.1, bf16[128,512]{1,0:T(8,128)(2,1)} %cot_ref.1), custom_call_target="tpu_custom_call" | custom-call | flops 4294967296 | bytes 8388608 | tf_op jit(solution)/shard_map/pallas_call | solution.py:333
  114.0 1.0 slice_reduce_fusion
  114.9 0.0 copy-done
  115.0 0.0 copy-start.2
  115.0 0.0 copy-start.1
  115.0 4.0 %multiply_convert_fusion = bf16[128,8192]{1,0:T(8,128)(2,1)} fusion(bf16[128,8192]{1,0:T(8,128)(2,1)S(1)} %copy-done, bf16[128,8192]{1,0:T(8,128)(2,1)} %get-tuple-element.9, f32[128]{0:T(128)S(1)} %get-tuple-element.13, f32[128]{0:T(128)S(1)} %get-tuple-element.14), kind=kLoop, calls=%fused_computation | loop fusion | flops 7340032 | bytes 6292480 | tf_op jit(solution)/shard_map/convert_element_type | solution.py:369
  118.9 0.0 copy-done.2
  118.9 0.6 convert_bitcast_fusion
  119.5 0.0 copy-done.1
  119.5 0.7 copy.8
Async XLA Ops:
  0.6 114.3 %copy-start = (bf16[128,8192]{1,0:T(8,128)(2,1)S(1)}, bf16[128,8192]{1,0:T(8,128)(2,1)}, u32[]{:S(2)}) copy-start(bf16[128,8192]{1,0:T(8,128)(2,1)} %x_ref.1) | copy-start | bytes 6291460
  115.0 4.0 %copy-start.2 = (f32[16,128]{1,0:T(8,128)S(1)}, f32[16,128]{1,0:T(8,128)}, u32[]{:S(2)}) copy-start(f32[16,128]{1,0:T(8,128)} %get-tuple-element.12) | copy-start | bytes 24580
  115.0 4.6 %copy-start.1 = (bf16[64,2048]{1,0:T(8,128)(2,1)S(1)}, bf16[64,2048]{1,0:T(8,128)(2,1)}, u32[]{:S(2)}) copy-start(bf16[64,2048]{1,0:T(8,128)(2,1)} %get-tuple-element.11) | copy-start | bytes 786436

commit v5 on v4

--- a/solution.py
+++ b/solution.py
@@ -60,8 +60,8 @@
 def kernel(
     n_d, n_f, n_k,
     x_ref, gain_ref, w_ref, cot_ref,
-    hat_ref, inv, mean_ref, wu_ref, gu_ref,
-    nb, cols, cot_all, gain_all, wall, gsend, slabs, cot_turned, products, g_own, g_all, gram1, gram2,
+    ig_ref, wu_ref, gu_ref,
+    inv, means, nb, cols, cot_all, gain_all, wall, gsend, slabs, cot_turned, products, g_own, g_all, gram1, gram2,
     w_send, w_recv, c_send, c_recv, n_send, n_recv, col_send, col_recv, hyp_send, hyp_recv,
     slab_send, slab_recv, g_send, g_recv, one_send, one_recv, two_send, two_recv,
 ):
@@ -136,15 +136,18 @@
 
     col_copies = []
 
-    def send_columns(k):
-        copies = []
+    for k in range(n_k):
         for o in range(n_f):
             normed = (x_ref[:, features(o, k)].astype(F32) * inv[:, :1]).astype(BF16)
             if o == 0:
                 cols[k, 0] = normed
-                continue
+            else:
+                nb[k, o - 1] = normed
+
+    def send_columns(k):
+        copies = []
+        for o in range(1, n_f):
             at = n_f - o
-            nb[k, o - 1] = normed
             copies.append(
                 send(nb.at[k, o - 1], cols.at[k, at], col_send.at[k, o - 1], col_recv.at[k, at - 1], f_peer(o))
             )
@@ -197,12 +200,23 @@
             for k in range(n_k):
                 hat = back_part(o, k)
                 place = features(o, k)
-                hat_ref[:, place] = hat
+                ig_ref[:, place] = hat
                 term = hat.astype(F32) * (x_ref[:, place].astype(F32) * inv[:, :1])
                 for at in range(0, chunk, 128):
                     total = total + term[:, at : at + 128]
         mean_term = jnp.sum(total, axis=1, keepdims=True) / model
-        mean_ref[...] = jnp.broadcast_to(mean_term, mean_ref.shape)
+        means[...] = jnp.broadcast_to(mean_term, means.shape)
+
+    def finish(part):
+        def step(at, carry):
+            place = pl.ds(pl.multiple_of(at * 512, 512), 512)
+            normed = x_ref[:, place].astype(F32) * inv[:, :1]
+            hat32 = ig_ref[:, place].astype(F32)
+            ig_ref[:, place] = (inv[:, :1] * (hat32 - normed * means[:, :1])).astype(BF16)
+            return carry
+
+        blocks = model // 512
+        lax.fori_loop(part * blocks // 2, (part + 1) * blocks // 2, step, 0)
 
     slab_copies = []
 
@@ -216,11 +230,12 @@
             products[...] += dot_t(block, block)
 
     levels = len(bits)
+    spread(0)
     send_columns(0)
     if n_k > 1:
         send_columns(1)
-    spread(0)
-    done = 0
+    spread(1)
+    done = 1
     for copy in cot_copies + gain_copies:
         copy.wait_recv()
     cot_turned[...] = cot_all[...].reshape(n_f * tok, width).T
@@ -249,7 +264,7 @@
         back = dot_t(cotangent, w_ref[place])
         gain_grad = jnp.sum(back * columns32, axis=0, keepdims=True) * scale
         g_own[:, place] = gain_grad.astype(BF16).astype(F32)
-        if done < levels:
+        if 0 < k < n_k - 1 and done < levels:
             done += 1
             spread(done)
         if k:
@@ -280,6 +295,7 @@
         one_copies.append(
             send(gram1.at[d], gram1.at[d], one_send.at[o - 1], one_recv.at[n_d - o - 1], d_peer(o))
         )
+    finish(0)
     for copy in g_copies:
         copy.wait_recv()
     gains = g_all[...].reshape(n_d, owned)
@@ -299,6 +315,7 @@
         two_copies.append(
             send(gram2.at[f], gram2.at[f], two_send.at[o - 1], two_recv.at[n_f - o - 1], f_peer(o))
         )
+    finish(1)
     for copy in two_copies:
         copy.wait_recv()
     sum_w, sum_g = gram2[0, 0], gram2[0, 1]
@@ -330,18 +347,18 @@
     vmem = pl.BlockSpec(memory_space=pltpu.VMEM)
     pairs = [(n_f - 1,)] * 6 + [(n_k, n_f - 1)] * 2 + [(2, n_d - 1)] * 2 + [(n_k, n_d - 1)] * 2
     pairs += [(n_d - 1,)] * 4 + [(n_f - 1,)] * 2
-    hat, inverse_rms, mean_term, weight, gain = pl.pallas_call(
+    input_grad, weight, gain = pl.pallas_call(
         functools.partial(kernel, n_d, n_f, n_k),
         out_shape=(
             jax.ShapeDtypeStruct((tok, model), BF16),
-            jax.ShapeDtypeStruct((tok, 128), F32),
-            jax.ShapeDtypeStruct((tok, 128), F32),
             jax.ShapeDtypeStruct((slab, owned), BF16),
             jax.ShapeDtypeStruct((owned // 128, 128), F32),
         ),
         in_specs=[vmem] * 4,
-        out_specs=(vmem,) * 5,
+        out_specs=(vmem,) * 3,
         scratch_shapes=[
+            pltpu.VMEM((tok, 128), F32),
+            pltpu.VMEM((tok, 128), F32),
             pltpu.VMEM((n_k, n_f - 1, tok, chunk), BF16),
             pltpu.VMEM((n_k, n_f, tok, chunk), BF16),
             pltpu.VMEM((n_f, tok, width), BF16),
@@ -364,9 +381,6 @@
             flops=8 * tok * model * width, bytes_accessed=8 * tok * model, transcendentals=0
         ),
     )(layer_input, norm_gain.reshape(1, owned), value_weight, value_cotangent)
-    inverse_rms = inverse_rms[:, :1]
-    normed = layer_input.astype(F32) * inverse_rms
-    input_grad = (inverse_rms * (hat.astype(F32) - normed * mean_term[:, :1])).astype(BF16)
     return (input_grad, weight.T, gain.reshape(owned).astype(BF16))
 
 

time: 120 us -> 113 us (0.942)
  Pallas kernels: 113 us -> 107 us
  other arithmetic: 4.55 us -> 1.29 us
  local copies, waits for them, and re-layouts: 1.69 us -> 3.84 us
    pallas_call x1, Pallas kernels: 113 us -> 107 us  [body(): pl.pallas_call(functools.partial(kernel, n_d, n_f, n_k), out_shape=(jax.S...]
    convert_element_type x1 -> x0, other arithmetic: 3.96 us -> none  [body(): (inverse_rms * (hat.astype(F32) - normed * mean_term[:, :1])).astype(BF16)]
    unnamed x7 -> x4, local copies, waits for them, and re-layouts: 0.72 us -> 3.84 us
where the time goes in v5:
time: 113 us
  Pallas kernels  107 us (95%)
  local copies, waits for them, and re-layouts  3.84 us (3%)
  other arithmetic  1.29 us (1%)
    pallas_call x1, Pallas kernels, body(): pl.pallas_call(functools.partial(kernel, n_d, n_f, n_k), out_shape=(jax.S...  107 us
    unnamed x4, local copies, waits for them, and re-layouts  3.84 us

profile of v5, /device:TPU:0, one launch (start us, length us, event | category | flops | bytes accessed | tf_op | source)
XLA Modules:
  0.0 113.1 jit_solution(15526519584105356699)
XLA Ops:
  0.6 107.4 %shard_map.67 = (bf16[128,8192]{1,0:T(8,128)(2,1)}, bf16[64,2048]{1,0:T(8,128)(2,1)}, f32[16,128]{1,0:T(8,128)}) custom-call(bf16[128,8192]{1,0:T(8,128)(2,1)} %x_ref.1, f32[1,2048]{1,0:T(1,128)} %bitcast.5, bf16[2048,512]{1,0:T(8,128)(2,1)} %w_ref.1, bf16[128,512]{1,0:T(8,128)(2,1)} %cot_ref.1), custom_call_target="tpu_custom_call" | custom-call | flops 4294967296 | bytes 8388608 | tf_op jit(solution)/shard_map/pallas_call | solution.py:350
  108.0 1.3 %convert_bitcast_fusion = bf16[2048]{0:T(1024)(128)(2,1)} fusion(f32[16,128]{1,0:T(8,128)} %get-tuple-element.8), kind=kLoop, calls=%fused_computation | loop fusion | flops 2048 | bytes 12288 | tf_op jit(solution)/shard_map/convert_element_type | solution.py:384
  109.3 0.0 copy-start
  109.3 3.1 %copy.9 = bf16[128,8192]{1,0:T(8,128)(2,1)} copy(bf16[128,8192]{1,0:T(8,128)(2,1)} %get-tuple-element.12) | data formatting | bytes 4194304
  112.4 0.0 copy-done
  112.4 0.7 copy.10
Async XLA Ops:
  109.3 3.1 %copy-start = (bf16[64,2048]{1,0:T(8,128)(2,1)S(1)}, bf16[64,2048]{1,0:T(8,128)(2,1)}, u32[]{:S(2)}) copy-start(bf16[64,2048]{1,0:T(8,128)(2,1)} %get-tuple-element.7) | copy-start | bytes 786436

commit v6 on v5

--- a/solution.py
+++ b/solution.py
@@ -61,7 +61,7 @@
     n_d, n_f, n_k,
     x_ref, gain_ref, w_ref, cot_ref,
     ig_ref, wu_ref, gu_ref,
-    inv, means, nb, cols, cot_all, gain_all, wall, gsend, slabs, cot_turned, products, g_own, g_all, gram1, gram2,
+    inv, means, cot_plane, hat_out, hat_in, p_send, p_recv, h_send, h_recv, nb, cols, cot_all, gain_all, wall, gsend, slabs, cot_turned, products, g_own, g_all, gram1, gram2,
     w_send, w_recv, c_send, c_recv, n_send, n_recv, col_send, col_recv, hyp_send, hyp_recv,
     slab_send, slab_recv, g_send, g_recv, one_send, one_recv, two_send, two_recv,
 ):
@@ -72,6 +72,7 @@
     rows = owned // n_d
     slab = width // n_d
     scale = 1.0 / math.sqrt(n_f * tok)
+    direct = rows % 128 == 0
     sent = []
 
     def f_peer(o):
@@ -120,6 +121,13 @@
         gain_copies.append(
             send(gain_ref, gain_all.at[at], n_send.at[o - 1], n_recv.at[at - 1], f_peer(o))
         )
+    plane_copies = []
+    if direct:
+        for o in range(1, n_d):
+            plane_copies.append(
+                send(cot_ref, cot_plane.at[d], p_send.at[o - 1], p_recv.at[n_d - o - 1], d_peer(o))
+            )
+        cot_plane[d] = cot_ref[...]
     cot_all[0] = cot_ref[...]
     gain_all[0] = gain_ref[...]
 
@@ -185,6 +193,39 @@
                     )
                 )
 
+    hat_copies = []
+
+    def send_hats():
+        for copy in plane_copies:
+            copy.wait_recv()
+        tokens = cot_plane[...].reshape(n_d * tok, width)
+        for o in range(n_f):
+            block = w_ref[own_rows] if o == 0 else wall[d, o - 1]
+            own_gain = gain_all[o, :, pl.ds(pl.multiple_of(d * rows, 128), rows)]
+            hat = (dot_t(tokens, block) * own_gain).astype(BF16)
+            hat_out[:, o] = hat.reshape(n_d, tok, rows)
+        for o in range(1, n_d):
+            hat_copies.append(
+                send(
+                    hat_out.at[lax.rem(d + o, n_d)], hat_in.at[d], h_send.at[o - 1], h_recv.at[n_d - o - 1], d_peer(o),
+                )
+            )
+        hat_in[d] = hat_out[d]
+
+    def place_hats():
+        for copy in hat_copies:
+            copy.wait_recv()
+        total = jnp.zeros((tok, 128), F32)
+        for s in range(n_d):
+            for o in range(n_f):
+                place = pl.ds(pl.multiple_of(lax.rem(f + o, n_f) * owned + s * rows, 128), rows)
+                hat = hat_in[s, o]
+                ig_ref[:, place] = hat
+                term = hat.astype(F32) * (x_ref[:, place].astype(F32) * inv[:, :1])
+                for at in range(0, rows, 128):
+                    total = total + term[:, at : at + 128]
+        means[...] = jnp.broadcast_to(jnp.sum(total, axis=1, keepdims=True) / model, means.shape)
+
     def hat_gradient():
         def back_part(o, k):
             if o == 0:
@@ -230,13 +271,24 @@
             products[...] += dot_t(block, block)
 
     levels = len(bits)
-    spread(0)
-    send_columns(0)
-    if n_k > 1:
-        send_columns(1)
-    spread(1)
-    done = 1
-    for copy in cot_copies + gain_copies:
+    if direct:
+        send_columns(0)
+        for copy in first + gain_copies:
+            copy.wait_recv()
+        if n_k > 1:
+            send_columns(1)
+        send_hats()
+        done = levels
+    else:
+        spread(0)
+        send_columns(0)
+        if n_k > 1:
+            send_columns(1)
+        spread(1)
+        done = 1
+        for copy in gain_copies:
+            copy.wait_recv()
+    for copy in cot_copies:
         copy.wait_recv()
     cot_turned[...] = cot_all[...].reshape(n_f * tok, width).T
     for k in range(n_k):
@@ -277,7 +329,7 @@
     while done < levels:
         done += 1
         spread(done)
-    hat_gradient()
+    place_hats() if direct else hat_gradient()
     gather_products(n_k - 1)
 
     row = lax.broadcasted_iota(jnp.int32, (width, width), 0)
@@ -344,6 +396,7 @@
     n_k = owned // chunk
     rows, slab = owned // n_d, width // n_d
     dma = pltpu.SemaphoreType.DMA
+    hat_shape = (n_d, n_f, tok, rows) if rows % 128 == 0 else (1, 1, 16, 128)
     vmem = pl.BlockSpec(memory_space=pltpu.VMEM)
     pairs = [(n_f - 1,)] * 6 + [(n_k, n_f - 1)] * 2 + [(2, n_d - 1)] * 2 + [(n_k, n_d - 1)] * 2
     pairs += [(n_d - 1,)] * 4 + [(n_f - 1,)] * 2
@@ -359,6 +412,10 @@
         scratch_shapes=[
             pltpu.VMEM((tok, 128), F32),
             pltpu.VMEM((tok, 128), F32),
+            pltpu.VMEM((n_d, tok, width), BF16),
+            pltpu.VMEM(hat_shape, BF16),
+            pltpu.VMEM(hat_shape, BF16),
+            *[dma((n_d - 1,))] * 4,
             pltpu.VMEM((n_k, n_f - 1, tok, chunk), BF16),
             pltpu.VMEM((n_k, n_f, tok, chunk), BF16),
             pltpu.VMEM((n_f, tok, width), BF16),

time: 113 us -> 114 us (level)
  no operation moved by 1% of the time
where the time goes in v6:
time: 114 us
  Pallas kernels  108 us (95%)
  local copies, waits for them, and re-layouts  3.84 us (3%)
  other arithmetic  1.29 us (1%)
    pallas_call x1, Pallas kernels, body(): pl.pallas_call(functools.partial(kernel, n_d, n_f, n_k), out_shape=(jax.S...  108 us
    unnamed x4, local copies, waits for them, and re-layouts  3.84 us

profile of v6, /device:TPU:0, one launch (start us, length us, event | category | flops | bytes accessed | tf_op | source)
XLA Modules:
  0.0 114.1 jit_solution(2915850118686078946)
XLA Ops:
  0.6 108.4 %shard_map.67 = (bf16[128,8192]{1,0:T(8,128)(2,1)}, bf16[64,2048]{1,0:T(8,128)(2,1)}, f32[16,128]{1,0:T(8,128)}) custom-call(bf16[128,8192]{1,0:T(8,128)(2,1)} %x_ref.1, f32[1,2048]{1,0:T(1,128)} %bitcast.5, bf16[2048,512]{1,0:T(8,128)(2,1)} %w_ref.1, bf16[128,512]{1,0:T(8,128)(2,1)} %cot_ref.1), custom_call_target="tpu_custom_call" | custom-call | flops 4294967296 | bytes 8388608 | tf_op jit(solution)/shard_map/pallas_call | solution.py:403
  109.0 1.3 %convert_bitcast_fusion = bf16[2048]{0:T(1024)(128)(2,1)} fusion(f32[16,128]{1,0:T(8,128)} %get-tuple-element.8), kind=kLoop, calls=%fused_computation | loop fusion | flops 2048 | bytes 12288 | tf_op jit(solution)/shard_map/convert_element_type | solution.py:441
  110.3 0.0 copy-start
  110.3 3.1 %copy.9 = bf16[128,8192]{1,0:T(8,128)(2,1)} copy(bf16[128,8192]{1,0:T(8,128)(2,1)} %get-tuple-element.12) | data formatting | bytes 4194304
  113.4 0.0 copy-done
  113.4 0.7 copy.10
Async XLA Ops:
  110.3 3.1 %copy-start = (bf16[64,2048]{1,0:T(8,128)(2,1)S(1)}, bf16[64,2048]{1,0:T(8,128)(2,1)}, u32[]{:S(2)}) copy-start(bf16[64,2048]{1,0:T(8,128)(2,1)} %get-tuple-element.7) | copy-start | bytes 786436
